TPU v7x, 256 devices: a whole 4x4x8 slice. The times are simulated.
256 devices in a mesh: ctx: 16 (over z, core), ep: 16 (over x, y).
Axes of the slice: x: 4, y: 4, z: 8, core: 2. Of those that a mesh axis runs over, the one named last changes fastest.
Arguments:
- residual: bfloat16 [16384, 2048], P(('ctx', 'ep')), may hold values from -6 to 6
- query_states: bfloat16 [16384, 2048], P('ctx', 'ep'), may hold values from -5 to 5
- key_states: bfloat16 [16384, 512], P('ctx'), may hold values from -5 to 5
- value_states: bfloat16 [16384, 512], P('ctx'), may hold values from -6 to 6
- out_proj: bfloat16 [2048, 2048], P('ep'), may hold values from -0.125 to 0.125
- norm_gain: float32 [2048], replicated, may hold values from 0.25 to 1.75
- w_gate: bfloat16 [256, 2048, 384], P(('ctx', 'ep')), may hold values from -0.125 to 0.125
- w_up: bfloat16 [256, 2048, 384], P(('ctx', 'ep')), may hold values from -0.125 to 0.125
- w_down: bfloat16 [256, 384, 2048], P(('ctx', 'ep')), may hold values from -0.21875 to 0.21875
- expert_ids: int32 [16384, 8], P(('ctx', 'ep')), may hold values from 0 to 127, all different within a row; in each aligned block of 64 rows (0 to 63, 64 to 127, ...) at most 6 rows name the same one
- route_weights: float32 [16384, 8], P(('ctx', 'ep')), may hold values from 0.05 to 1
Outputs:
- layer_out: bfloat16 [16384, 2048], P(('ctx', 'ep'))
Inputs may be any that keep to these rules, and one draw needn't show every extreme that they name: `expert_ids`: among the rows of one device no expert is named more than 6 times.
All inputs are finite; a program needn't handle non-finite values.
Results may differ from a plain program's by a relative error of at most 0.018.
Values may be sent and summed in bfloat16 or wider, within the bound.
No kernel may reach another device: no remote copies, remote signals or barrier semaphores. Data moves between devices by JAX's collectives and lax.ppermute only.
A program may use at most 64 MiB of HBM per device.

v0:
```python
import math

import jax
import jax.numpy as jnp
from jax import lax
from jax.sharding import PartitionSpec as P

D = 2048
HD = 128
KVH = 4
HQ = 16
EXPERTS = 128
CAP = 6


def folded_position(index, tok_ctx, n_ctx):
    half_rows = tok_ctx // 2
    shard = index // tok_ctx
    within = index % tok_ctx
    block = jnp.where(within < half_rows, shard, 2 * n_ctx - 1 - shard)
    return block * half_rows + within % half_rows


def expert_apply(arrived, w_gate, w_up, w_down):
    gate_acts = jnp.einsum("abrcd,rdh->abrch", arrived, w_gate, preferred_element_type=jnp.float32)
    up_acts = jnp.einsum("abrcd,rdh->abrch", arrived, w_up, preferred_element_type=jnp.float32)
    hidden = (jax.nn.silu(gate_acts) * up_acts).astype(jnp.bfloat16)
    return jnp.einsum(
        "abrch,rhd->abrcd", hidden, w_down, preferred_element_type=jnp.float32
    ).astype(jnp.bfloat16)


def shards(
    residual,
    query_states,
    key_states,
    value_states,
    out_proj,
    norm_gain,
    w_gate,
    w_up,
    w_down,
    expert_ids,
    route_weights,
):
    n_ctx = lax.axis_size("ctx")
    n_ep = lax.axis_size("ep")
    tok_ctx = query_states.shape[0]
    heads_dev = query_states.shape[1] // HD
    half_rows = tok_ctx // 2
    group_size = HQ // KVH
    score_scale = 1.0 / math.sqrt(HD)
    ctx_index = lax.axis_index("ctx")
    ep_index = lax.axis_index("ep")
    kv_head = ep_index * heads_dev // group_size
    key_head = lax.dynamic_slice_in_dim(key_states, kv_head * HD, HD, 1)
    value_head = lax.dynamic_slice_in_dim(value_states, kv_head * HD, HD, 1)
    own_pos = folded_position(
        ctx_index * tok_ctx + jnp.arange(tok_ctx, dtype=jnp.int32), tok_ctx, n_ctx
    ).reshape(2, half_rows)
    query_blocks = query_states.reshape(2, half_rows, heads_dev, HD)
    start_state = (
        jnp.full((heads_dev, half_rows), -1e30, jnp.float32),
        jnp.zeros((heads_dev, half_rows), jnp.float32),
        jnp.zeros((heads_dev, half_rows, HD), jnp.float32),
    )
    key_piece = lax.all_gather(key_head, "ctx", axis=0, tiled=True)
    value_piece = lax.all_gather(value_head, "ctx", axis=0, tiled=True)
    count = key_piece.shape[0]

    def one_sub(number, state_pair):
        first = (number * half_rows).astype(jnp.int32)
        key_sub = lax.dynamic_slice_in_dim(key_piece, first, half_rows, 0)
        value_sub = lax.dynamic_slice_in_dim(value_piece, first, half_rows, 0)
        key_pos = folded_position(first + jnp.arange(half_rows, dtype=jnp.int32), tok_ctx, n_ctx)
        updated = []
        for half in range(2):
            query_pos = own_pos[half]

            def update(state):
                run_max, run_total, run_acc = state
                scores = (
                    jnp.einsum(
                        "bhd,nd->hbn",
                        query_blocks[half],
                        key_sub,
                        preferred_element_type=jnp.float32,
                    )
                    * score_scale
                )
                allowed = (key_pos[None, :] <= query_pos[:, None])[None]
                scores = jnp.where(allowed, scores, -1e30)
                new_max = jnp.maximum(run_max, jnp.max(scores, axis=2))
                weights = jnp.where(allowed, jnp.exp(scores - new_max[:, :, None]), 0.0)
                correction = jnp.exp(run_max - new_max)
                new_total = run_total * correction + jnp.sum(weights, axis=2)
                new_acc = run_acc * correction[:, :, None] + jnp.einsum(
                    "hbn,nd->hbd",
                    weights.astype(jnp.bfloat16),
                    value_sub,
                    preferred_element_type=jnp.float32,
                )
                return (new_max, new_total, new_acc)

            needed = jnp.min(key_pos) <= jnp.max(query_pos)
            updated.append(lax.cond(needed, update, lambda state: state, state_pair[half]))
        return (updated[0], updated[1])

    final_state = lax.fori_loop(0, count // half_rows, one_sub, (start_state, start_state))
    halves_out = jnp.stack(
        [final_state[half][2] / final_state[half][1][:, :, None] for half in range(2)]
    )
    attended = (
        halves_out.transpose(0, 2, 1, 3).reshape(tok_ctx, heads_dev * HD).astype(jnp.bfloat16)
    )
    projected = lax.psum_scatter(
        jnp.dot(attended, out_proj, preferred_element_type=jnp.float32).astype(jnp.bfloat16),
        "ep",
        scatter_dimension=0,
        tiled=True,
    ).astype(jnp.float32)
    stream = residual.astype(jnp.float32) + projected
    normed = (
        stream * lax.rsqrt(jnp.mean(stream * stream, axis=1, keepdims=True) + 1e-06) * norm_gain
    ).astype(jnp.bfloat16)
    tok_rows, top_count = expert_ids.shape
    flat_ids = expert_ids.reshape(-1)
    onehot = (flat_ids[:, None] == jnp.arange(EXPERTS, dtype=jnp.int32)[None, :]).astype(jnp.int32)
    earlier = jnp.cumsum(onehot, axis=0) - onehot
    slot_rank = jnp.sum(earlier * onehot, axis=1)
    slot_index = (flat_ids * CAP + slot_rank).reshape(tok_rows, top_count)
    all_slots = jnp.arange(EXPERTS * CAP, dtype=jnp.int32)
    select = jnp.sum(
        (slot_index[None, :, :] == all_slots[:, None, None]).astype(jnp.int32), axis=2
    ).astype(jnp.bfloat16)
    packed = (
        jnp.dot(select, normed, preferred_element_type=jnp.float32)
        .astype(jnp.bfloat16)
        .reshape(EXPERTS, CAP, D)
    )
    per_device = w_gate.shape[0]
    doubled = jnp.broadcast_to(packed[:, None], (EXPERTS, 2, CAP, D)).reshape(
        n_ctx, n_ep, per_device, CAP, D
    )
    arrived = lax.all_to_all(
        lax.all_to_all(doubled, "ctx", split_axis=0, concat_axis=0, tiled=True),
        "ep",
        split_axis=1,
        concat_axis=1,
        tiled=True,
    )
    results = expert_apply(arrived, w_gate, w_up, w_down)
    returned = lax.all_to_all(
        lax.all_to_all(results, "ctx", split_axis=0, concat_axis=0, tiled=True),
        "ep",
        split_axis=1,
        concat_axis=1,
        tiled=True,
    ).reshape(EXPERTS, 2, CAP, D)
    expert_out = (returned[:, 0].astype(jnp.float32) + returned[:, 1].astype(jnp.float32)).astype(
        jnp.bfloat16
    )
    picked = jnp.take(expert_out.reshape(EXPERTS * CAP, D), slot_index.reshape(-1), axis=0).astype(
        jnp.float32
    )
    expert_mix = jnp.sum(picked.reshape(tok_rows, top_count, D) * route_weights[:, :, None], axis=1)
    return (stream + expert_mix).astype(jnp.bfloat16)


def solution(mesh):
    return jax.shard_map(
        shards,
        mesh=mesh,
        in_specs=(
            P(("ctx", "ep"), None),
            P("ctx", "ep"),
            P("ctx", None),
            P("ctx", None),
            P("ep", None),
            P(),
            P(("ctx", "ep"), None, None),
            P(("ctx", "ep"), None, None),
            P(("ctx", "ep"), None, None),
            P(("ctx", "ep"), None),
            P(("ctx", "ep"), None),
        ),
        out_specs=P(("ctx", "ep"), None),
        check_vma=False,
    )
```

profile of v0, /device:TPU:96, one launch (start us, length us, event | category | flops | bytes accessed | tf_op | source)
XLA Modules:
  0.0 1001.6 jit_solution(7845107260201816931)
XLA Ops:
  10.9 41.6 %all-gather.3.cloned.1.call-done = bf16[16384,128]{1,0:T(8,128)(2,1)} async-done(((bf16[1024,128]{1,0:T(8,128)(2,1)}), bf16[16384,128]{1,0:T(8,128)(2,1)}) %all-gather.3.cloned.1.call-update) | async-done | bytes 4194320 | tf_op jit(solution)/shard_map/all_gather | solution.py:67
  52.4 42.5 %all-gather.5.cloned.1.call-done = bf16[16384,128]{1,0:T(8,128)(2,1)} async-done(((bf16[1024,128]{1,0:T(8,128)(2,1)}), bf16[16384,128]{1,0:T(8,128)(2,1)}) %all-gather.5.cloned.1.call-update) | async-done | bytes 4194320 | tf_op jit(solution)/shard_map/all_gather | solution.py:68
  95.1 203.4 %while.27 = (s32[]{:T(128)}, f32[1,512]{1,0:T(1,128)S(1)}, f32[1,512]{1,0:T(1,128)S(1)}, f32[1,512,128]{2,1,0:T(8,128)S(1)}, f32[1,512]{1,0:T(1,128)S(1)}, /*ind...) while((s32[]{:T(128)}, f32[1,512]{1,0:T(1,128)S(1)}, ...), condition=%wide.region_12.13_spmd.clone, body=%wide.region_2.12_spmd.clone.sunk | while | flops 275048960 | bytes 8755687 | solution.py:109
  304.3 79.8 %reduce-scatter.2.cloned.1.call-done = bf16[64,2048]{1,0:T(8,128)(2,1)} async-done(((bf16[1024,2048]{1,0:T(8,128)(2,1)}), bf16[64,2048]{1,0:T(8,128)(2,1)}) %reduce-scatter.2.cloned.1.call-update) | async-done | bytes 262160 | tf_op jit(solution)/shard_map/reduce_scatter | solution.py:116
  389.0 6.3 broadcast_in_dim.58
  395.2 3.9 copy.79
  399.1 5.2 broadcast_in_dim.59
  404.3 10.2 %reshape.265 = bf16[16,16,1,6,2048]{4,1,0,3,2:T(8,128)(2,1)} reshape(bf16[128,2,6,2048]{3,1,0,2:T(2,128)(2,1)} %broadcast_in_dim.59) | data formatting | bytes 12582912 | tf_op jit(solution)/shard_map/reshape | solution.py:142
  417.9 156.3 %all_to_all.20 = bf16[16,16,1,6,2048]{4,1,3,2,0:T(8,128)(2,1)S(1)} all-to-all(bf16[16,16,1,6,2048]{4,1,3,2,0:T(8,128)(2,1)S(1)} %copy.80), channel_id=1, replica_groups=mesh['ctx'=16,'ep'=16] {'ctx'}, dimensions={0} | all-to-all | bytes 12582912 | tf_op jit(solution)/shard_map/all_to_all | solution.py:146
  577.6 78.5 %all_to_all.21 = bf16[16,16,1,6,2048]{4,0,3,2,1:T(8,128)(2,1)S(1)} all-to-all(bf16[16,16,1,6,2048]{4,0,3,2,1:T(8,128)(2,1)S(1)} %copy.81), channel_id=1, replica_groups=mesh['ctx'=16,'ep'=16] {'ep'}, dimensions={1} | all-to-all | bytes 12582912 | tf_op jit(solution)/shard_map/all_to_all | solution.py:145
  656.1 5.9 fusion.39
  662.0 5.9 fusion.52
  667.9 4.1 convert_bitcast_fusion
  672.0 143.5 %all_to_all.22 = bf16[16,16,1,6,2048]{4,1,3,2,0:T(8,128)(2,1)S(1)} all-to-all(bf16[16,16,1,6,2048]{4,1,3,2,0:T(8,128)(2,1)S(1)} %convert_bitcast_fusion), channel_id=1, replica_groups=mesh['ctx'=16,'ep'=16] {'ctx'}, dimensions={0} | all-to-all | bytes 12582912 | tf_op jit(solution)/shard_map/all_to_all | solution.py:154
  815.5 6.1 copy.84
  821.6 4.8 all-to-all-start.3
  826.8 106.2 %all-to-all-done.3 = bf16[16,16,1,6,2048]{4,0,3,2,1:T(8,128)(2,1)} async-done(((bf16[16,16,1,6,2048]{4,0,3,2,1:T(8,128)(2,1)}), bf16[16,16,1,6,2048]{4,0,3,2,1:T(8,128)(2,1)}, u32[]{:S(2)}, u32[]{:S(2)}) %all-to-all-start.3) | async-done | bytes 6291488 | tf_op jit(solution)/shard_map/all_to_all | solution.py:153
  933.0 9.3 copy.85
  942.4 10.9 %reshape.271 = bf16[128,2,6,2048]{3,1,0,2:T(2,128)(2,1)} reshape(bf16[16,16,1,6,2048]{4,1,0,3,2:T(8,128)(2,1)} %copy.85) | data formatting | bytes 12582912 | tf_op jit(solution)/shard_map/reshape | solution.py:159
  953.2 12.9 %fusion.74 = (bf16[128,1,6,2048]{3,1,0,2:T(2,128)(2,1)S(1)}, bf16[128,1,6,2048]{3,1,0,2:T(2,128)(2,1)S(1)}) fusion(bf16[128,2,6,2048]{3,1,0,2:T(2,128)(2,1)} %reshape.271), kind=kLoop, calls=%fused_computation.141 | loop fusion | bytes 12582912 | tf_op jit(solution)/shard_map/slice | solution.py:160
  966.1 6.4 add_convert_fusion
  976.2 6.3 convert_element_type.117
  982.6 7.7 gather_fusion
  990.3 3.8 multiply_reduce_fusion
  (461 shorter events, 216.1 us)
Async XLA Ops:
  6.5 661.4 %copy-start = (bf16[1,384,2048]{2,1,0:T(8,128)(2,1)S(1)}, bf16[1,384,2048]{2,1,0:T(8,128)(2,1)}, u32[]{:S(2)}) copy-start(bf16[1,384,2048]{2,1,0:T(8,128)(2,1)} %param.25) | copy-start | bytes 4718596
  6.5 45.9 %all-gather.3.cloned.1.call-start = ((), (), s32[]{:S(2)}) async-start(), calls=%async_computation.5 | async-start | bytes 4456448 | tf_op jit(solution)/shard_map/all_gather | solution.py:67
  8.4 86.6 %all-gather.5.cloned.1.call-start = ((), (), s32[]{:S(2)}) async-start(), calls=%async_computation.6 | async-start | bytes 4456448 | tf_op jit(solution)/shard_map/all_gather | solution.py:68
  10.1 374.0 %reduce-scatter.2.cloned.1.call-start = ((), (), s32[]{:S(2)}) async-start(), calls=%async_computation.7 | async-start | bytes 4456448 | tf_op jit(solution)/shard_map/reduce_scatter | solution.py:116
  95.0 203.7 %copy-start.4 = (bf16[128,2048]{1,0:T(8,128)(2,1)S(1)}, bf16[128,2048]{1,0:T(8,128)(2,1)}, u32[]{:S(2)}) copy-start(bf16[128,2048]{1,0:T(8,128)(2,1)} %param.21) | copy-start | bytes 1572868
  301.9 0.7 copy-start.5
  301.9 82.2 %copy-start.2 = (bf16[64,2048]{1,0:T(8,128)(2,1)S(1)}, bf16[64,2048]{1,0:T(8,128)(2,1)}, u32[]{:S(2)}) copy-start(bf16[64,2048]{1,0:T(8,128)(2,1)} %param.17) | copy-start | bytes 786436
  301.9 83.4 %copy-start.6 = (f32[2048]{0:T(1024)S(1)}, f32[2048]{0:T(1024)}, u32[]{:S(2)}) copy-start(f32[2048]{0:T(1024)} %param.22) | copy-start | bytes 24580
  577.6 78.5 %copy-start.8 = (bf16[1,2048,384]{2,1,0:T(8,128)(2,1)S(1)}, bf16[1,2048,384]{2,1,0:T(8,128)(2,1)}, u32[]{:S(2)}) copy-start(bf16[1,2048,384]{2,1,0:T(8,128)(2,1)} %param.23) | copy-start | bytes 4718596
  656.1 5.9 copy-start.9
  821.6 5.1 copy-start.7
  821.6 111.4 %all-to-all-start.3 = ((bf16[16,16,1,6,2048]{4,0,3,2,1:T(8,128)(2,1)}), bf16[16,16,1,6,2048]{4,0,3,2,1:T(8,128)(2,1)}, u32[]{:S(2)}, u32[]{:S(2)}) async-start(bf16[16,16,1,6,2048]{4,0,3,2,1:T(8,128)(2,1)} %copy.84), calls=%async_computation.4 | async-start | bytes 12582912 | tf_op jit(solution)/shard_map/all_to_all | solution.py:153
  982.6 11.5 %copy-start.3 = (bf16[64,2048]{1,0:T(8,128)(2,1)S(1)}, bf16[64,2048]{1,0:T(8,128)(2,1)}, u32[]{:S(2)}) copy-start(bf16[64,2048]{1,0:T(8,128)(2,1)} %reduce-scatter.2.cloned.1.call-done) | copy-start | bytes 786436
  982.6 12.4 %copy-start.1 = (bf16[1,384,2048]{2,1,0:T(8,128)(2,1)S(1)}, bf16[1,384,2048]{2,1,0:T(8,128)(2,1)}, u32[]{:S(2)}) copy-start(bf16[1,384,2048]{2,1,0:T(8,128)(2,1)} %param.25) | copy-start | bytes 4718596
Sparse Core Ops, SparseCore 0:
  9.2 43.1 all-gather.2
  54.2 40.6 all-gather.4
  302.1 82.0 reduce-scatter.1
where the time goes:
time: 1010 us; the launch traced here: 1000 us
  blocking collectives  378 us (37%)
  waiting for transfers between devices  270 us (27%)
  local copies, waits for them, and re-layouts  127 us (13%)
  loops' own time  82.8 us (8%)
  matrix products  80.7 us (8%)
  other arithmetic  44.8 us (4%)
  between operations  13.6 us (1%)
    all_to_all x1, blocking collectives, shards(): lax.all_to_all(doubled, 'ctx', split_axis=0, concat_axis=0, tiled=True)  156 us
    all_to_all x1, blocking collectives, shards(): lax.all_to_all(results, 'ctx', split_axis=0, concat_axis=0, tiled=True)  144 us
    all_to_all x1, waiting for transfers between devices, shards(): lax.all_to_all(lax.all_to_all(results, 'ctx', split_axis=0, concat_axis=0...  106 us
    another operation x1, loops' own time, shards(): lax.fori_loop(0, count // half_rows, one_sub, (start_state, start_state))  80.8 us
    reduce_scatter x1, waiting for transfers between devices, shards(): lax.psum_scatter(jnp.dot(attended, out_proj, preferred_element_type=jnp.f...  79.8 us
    all_to_all x1, blocking collectives, shards(): lax.all_to_all(lax.all_to_all(doubled, 'ctx', split_axis=0, concat_axis=0...  78.5 us
    all_gather x1, waiting for transfers between devices, shards(): value_piece = lax.all_gather(value_head, 'ctx', axis=0, tiled=True)  42.5 us
    all_gather x1, waiting for transfers between devices, shards(): key_piece = lax.all_gather(key_head, 'ctx', axis=0, tiled=True)  41.6 us
  transfers between devices with their start and end apart: 4, of which 4 were waited for; matrix products, arithmetic and copies ran while one was open for 0% of the time, Pallas kernels for 0%

commit v1 on v0

v1 whole, which is shorter than its diff:
```python
import functools
import math

import jax
import jax.numpy as jnp
from jax import lax
from jax.experimental import pallas as pl
from jax.experimental.pallas import tpu as pltpu
from jax.sharding import PartitionSpec as P

D = 2048
HD = 128
KVH = 4
HQ = 16
EXPERTS = 128
TOP = 8
CAP = 6
ROWS = 512
CORES = 2
BF = jnp.bfloat16
F32 = jnp.float32
LOG2_SCALE = math.log2(math.e) / math.sqrt(HD)


def attention_step(shards_in, first, last, *refs):
    ids_ref, q_ref = refs[0], refs[1]
    kv_refs = refs[2 : 2 + shards_in]
    rest = refs[2 + shards_in :]
    if first:
        m_in = l_in = a_in = None
    else:
        m_in, l_in, a_in = rest[:3]
        rest = rest[3:]
    if last:
        out_ref, m_ref, l_ref, a_ref = rest
    else:
        m_ref, l_ref, a_ref = rest
    own = ids_ref[0]
    if not first:
        m_ref[...] = m_in[...]
        l_ref[...] = l_in[...]
        a_ref[...] = a_in[...]

    def start_of(half):
        return half * ROWS if isinstance(half, int) else pl.multiple_of(half * ROWS, ROWS)

    def tile(slot, half, kv_ref, part, fresh, diagonal):
        query = q_ref[pl.ds(start_of(half), ROWS)]
        offset = start_of(part)
        key = kv_ref[pl.ds(offset, ROWS)]
        value = kv_ref[pl.ds(2 * ROWS + offset, ROWS)]
        scores = (
            lax.dot_general(key, query, (((1,), (1,)), ((), ())), preferred_element_type=F32)
            * LOG2_SCALE
        )
        if diagonal:
            key_at = lax.broadcasted_iota(jnp.int32, scores.shape, 0)
            query_at = lax.broadcasted_iota(jnp.int32, scores.shape, 1)
            scores = jnp.where(key_at <= query_at, scores, -1e30)
        top = jnp.max(scores, axis=0, keepdims=True)
        if not fresh:
            old = m_ref[slot]
            top = jnp.maximum(old, top)
            correction = jnp.exp2(old - top)
        weights = jnp.exp2(scores - top)
        total = jnp.sum(weights, axis=0, keepdims=True)
        mixed = lax.dot_general(
            value, weights.astype(BF), (((0,), (0,)), ((), ())), preferred_element_type=F32
        )
        if not fresh:
            total = l_ref[slot] * correction + total
            mixed = a_ref[slot] * correction + mixed
        m_ref[slot] = top
        l_ref[slot] = total
        a_ref[slot] = mixed

    for at in range(shards_in):
        if first and at == 0:
            tile(0, 0, kv_refs[0], 0, True, True)
            tile(1, 1, kv_refs[0], 1, True, True)
            tile(2, 1, kv_refs[0], 0, True, False)
            continue
        early = ids_ref[1 + at] < own
        half = jnp.where(early, 0, 1)
        tile(2, 1, kv_refs[at], 0, False, False)
        tile(half, half, kv_refs[at], jnp.where(early, 0, 1), False, False)
    if last:
        out_ref[0:ROWS] = (a_ref[0] / l_ref[0]).T.astype(BF)
        top = jnp.maximum(m_ref[1], m_ref[2])
        one = jnp.exp2(m_ref[1] - top)
        two = jnp.exp2(m_ref[2] - top)
        mixed = a_ref[1] * one + a_ref[2] * two
        out_ref[ROWS : 2 * ROWS] = (mixed / (l_ref[1] * one + l_ref[2] * two)).T.astype(BF)


def attend(ids, query, shards_kv, state, last):
    first = state is None
    count = len(shards_kv)
    vmem = pl.BlockSpec(memory_space=pltpu.VMEM)
    state_shapes = ((3, 1, ROWS), (3, 1, ROWS), (3, HD, ROWS))
    operands = [ids, query, *shards_kv] + ([] if first else list(state))
    if last:
        out_shape = jax.ShapeDtypeStruct(query.shape, BF)
        out_specs = vmem
        scratch = [pltpu.VMEM(shape, F32) for shape in state_shapes]
    else:
        out_shape = [jax.ShapeDtypeStruct(shape, F32) for shape in state_shapes]
        out_specs = [vmem] * 3
        scratch = []
    tiles = 2 * count + (1 if first else 0)
    return pl.pallas_call(
        functools.partial(attention_step, count, first, last),
        out_shape=out_shape,
        in_specs=[pl.BlockSpec(memory_space=pltpu.SMEM)] + [vmem] * (len(operands) - 1),
        out_specs=out_specs,
        scratch_shapes=scratch,
        compiler_params=pltpu.CompilerParams(vmem_limit_bytes=32 << 20),
        cost_estimate=pl.CostEstimate(
            flops=tiles * 4 * ROWS * ROWS * HD,
            bytes_accessed=count * 4 * ROWS * HD * 2 + 2 * ROWS * HD * 2,
            transcendentals=tiles * ROWS * ROWS,
        ),
    )(*operands)


def shards(
    residual,
    query_states,
    key_states,
    value_states,
    out_proj,
    norm_gain,
    w_gate,
    w_up,
    w_down,
    expert_ids,
    route_weights,
):
    n_ctx = lax.axis_size("ctx")
    n_ep = lax.axis_size("ep")
    planes = n_ctx // CORES
    tok = residual.shape[0]
    local_experts = EXPERTS // n_ctx
    ctx_index = lax.axis_index("ctx")
    ep_index = lax.axis_index("ep")
    plane, core = ctx_index // CORES, ctx_index % CORES
    kv_head = ep_index * KVH // n_ep
    far = planes // 2

    def z_perm(step):
        return [
            (z * CORES + c, ((z + step) % planes) * CORES + c)
            for z in range(planes)
            for c in range(CORES)
        ]

    up_perm, down_perm = z_perm(1), z_perm(-1)
    core_perm = [(i, i ^ 1) for i in range(n_ctx)]
    pair_perm = [(i, i ^ 1) for i in range(n_ep)]

    def up(x):
        return lax.ppermute(x, "ctx", up_perm)

    def down(x):
        return lax.ppermute(x, "ctx", down_perm)

    def across(x):
        return lax.ppermute(x, "ctx", core_perm)

    def ring(x):
        rows = x.shape[0] // 2
        blocks = [x]
        above = below = x
        for _ in range(far - 1):
            above, below = up(above), down(below)
            blocks += [above, below]
        blocks.append(jnp.concatenate([up(above[:rows]), down(below[rows:])], axis=0))
        return blocks

    offsets = [0]
    for step in range(1, far):
        offsets += [-step, step]
    offsets.append(far)

    def shard_id(offset, other):
        return ((plane + offset) % planes) * CORES + jnp.bitwise_xor(core, other)

    key_head = lax.dynamic_slice_in_dim(key_states, kv_head * HD, HD, 1)
    value_head = lax.dynamic_slice_in_dim(value_states, kv_head * HD, HD, 1)
    kv_blocks = ring(jnp.concatenate([key_head, value_head], axis=0))

    gates = (w_gate[0], lax.ppermute(w_gate[0], "ep", pair_perm))
    ups = (w_up[0], lax.ppermute(w_up[0], "ep", pair_perm))
    downs = (w_down[0], lax.ppermute(w_down[0], "ep", pair_perm))
    columns = D // CORES
    proj_mine = lax.all_gather(
        lax.dynamic_slice_in_dim(out_proj, core * columns, columns, 1), "ep", axis=0, tiled=True
    )
    proj_other = across(proj_mine)
    routing = lax.all_gather(
        jnp.concatenate([expert_ids.astype(F32), route_weights], axis=1), "ctx", axis=0
    )

    state = None
    groups = [[0]] + [[1 + 2 * s, 2 + 2 * s] for s in range(far - 1)] + [[2 * far - 1]]
    for number, group in enumerate(groups):
        held, ids = [], [ctx_index]
        for at in group:
            held += [kv_blocks[at], across(kv_blocks[at])]
            ids += [shard_id(offsets[at], 0), shard_id(offsets[at], 1)]
        state = attend(
            jnp.stack(ids).astype(jnp.int32), query_states, held, state, number == len(groups) - 1
        )
    attended = state

    heads = lax.all_to_all(
        attended.reshape(n_ep, tok, HD), "ep", split_axis=0, concat_axis=0, tiled=True
    )
    heads = heads.transpose(1, 0, 2).reshape(tok, HQ * HD)
    mine = jnp.dot(heads, proj_mine, preferred_element_type=F32)
    other = jnp.dot(heads, proj_other, preferred_element_type=F32)
    projected = jnp.where(
        core == 0,
        jnp.concatenate([mine, other], axis=1),
        jnp.concatenate([other, mine], axis=1),
    )
    stream = residual.astype(F32) + projected
    normed = (
        stream * lax.rsqrt(jnp.mean(stream * stream, axis=1, keepdims=True) + 1e-06) * norm_gain
    ).astype(BF)

    order = jnp.stack([shard_id(offset, other) for offset in offsets for other in range(CORES)])
    routing = jnp.take(routing, order, axis=0)
    ids = routing[:, :, :TOP].astype(jnp.int32)
    gains = routing[:, :, TOP:]
    experts = ctx_index * local_experts + jnp.arange(local_experts, dtype=jnp.int32)
    match = ids[:, :, :, None] == experts
    chosen = jnp.any(match, axis=2)
    weight = jnp.sum(jnp.where(match, gains[:, :, :, None], 0.0), axis=2)
    counts = chosen.astype(jnp.int32)
    rank = jnp.cumsum(counts, axis=1) - counts
    half = n_ctx // 2
    at_slot = jnp.logical_and(
        chosen[:, :, :, None], rank[:, :, :, None] == jnp.arange(CAP, dtype=jnp.int32)
    )
    placed = at_slot.reshape(2, half, tok, local_experts, CAP).transpose(0, 3, 1, 4, 2)
    same = jnp.eye(half, dtype=jnp.bool_)[None, None, :, None, :, None]
    select = jnp.where(same, placed[:, :, :, :, None, :], False)
    slots = local_experts * half * CAP
    scaled = weight.reshape(2, half, tok, local_experts).transpose(0, 3, 1, 2)
    spread = jnp.where(select, scaled[:, :, None, None, :, :], 0.0).reshape(2, slots, half * tok)
    select = select.reshape(2, slots, half * tok).astype(BF)
    spread_high = spread.astype(BF)
    spread_low = (spread - spread_high.astype(F32)).astype(BF)

    blocks = []
    for block in ring(normed):
        blocks += [block, across(block)]
    packed = [
        jnp.dot(
            select[h],
            jnp.concatenate(blocks[h * half : (h + 1) * half], axis=0),
            preferred_element_type=F32,
        )
        .astype(BF)
        .reshape(local_experts, half * CAP, D)
        for h in range(2)
    ]
    packed = jnp.stack(packed, axis=1).reshape(n_ep, half * CAP, D)
    arrived = lax.all_to_all(packed, "ep", split_axis=0, concat_axis=0, tiled=True)
    arrived = arrived.reshape(n_ep * half * CAP, D)
    halves = []
    for h in range(2):
        gate_acts = jnp.dot(arrived, gates[h], preferred_element_type=F32)
        up_acts = jnp.dot(arrived, ups[h], preferred_element_type=F32)
        hidden = (jax.nn.silu(gate_acts) * up_acts).astype(BF)
        halves.append(jnp.dot(hidden, downs[h], preferred_element_type=F32).astype(BF))
    expert_out = (halves[0].astype(F32) + halves[1].astype(F32)).astype(BF)
    returned = lax.all_to_all(
        expert_out.reshape(n_ep, half * CAP, D), "ep", split_axis=0, concat_axis=0, tiled=True
    ).reshape(local_experts, 2, half * CAP, D)

    def contract(table, rows):
        return lax.dot_general(table, rows, (((0,), (0,)), ((), ())), preferred_element_type=F32)

    shares = []
    for h in range(2):
        rows = returned[:, h].reshape(slots, D)
        share = contract(spread_high[h], rows) + contract(spread_low[h], rows)
        shares.append(share.reshape(half // CORES, CORES, tok, D))
    shares = jnp.concatenate(shares, axis=0).astype(BF)
    crossed = across(shares[:, 1])
    sums = shares[:, 0].astype(F32) + crossed.astype(F32)
    at = {offset: number for number, offset in enumerate(offsets)}
    cut = D // 2
    going_down = down(sums[at[far], :, :cut].astype(BF))
    going_up = up(sums[at[far], :, cut:].astype(BF))
    for step in range(far - 1, 0, -1):
        low, high = sums[at[-step]], sums[at[step]]
        if step == far - 1:
            low = jnp.concatenate([low[:, :cut] + going_down.astype(F32), low[:, cut:]], axis=1)
            high = jnp.concatenate([high[:, :cut], high[:, cut:] + going_up.astype(F32)], axis=1)
        else:
            low = low + going_down.astype(F32)
            high = high + going_up.astype(F32)
        going_down, going_up = down(low.astype(BF)), up(high.astype(BF))
    mixture = sums[at[0]] + going_down.astype(F32) + going_up.astype(F32)
    return (stream + mixture).astype(BF)


def solution(mesh):
    return jax.shard_map(
        shards,
        mesh=mesh,
        in_specs=(
            P(("ctx", "ep"), None),
            P("ctx", "ep"),
            P("ctx", None),
            P("ctx", None),
            P("ep", None),
            P(),
            P(("ctx", "ep"), None, None),
            P(("ctx", "ep"), None, None),
            P(("ctx", "ep"), None, None),
            P(("ctx", "ep"), None),
            P(("ctx", "ep"), None),
        ),
        out_specs=P(("ctx", "ep"), None),
        check_vma=False,
    )
```

time: 1010 us -> 505 us (0.50)
  blocking collectives: 378 us -> 23 us
  local copies, waits for them, and re-layouts: 127 us -> 27 us
  loops' own time: 82.8 us -> 0 us
  starting transfers between devices: 4.84 us -> 60.3 us
  matrix products: 80.7 us -> 42 us
  other arithmetic: 44.8 us -> 11.5 us
  Pallas kernels: 0 us -> 23.8 us
  waiting for transfers between devices: 270 us -> 293 us
    all_to_all x3 -> x0, blocking collectives: 378 us -> none  [the longest x1 156 us: shards(): lax.all_to_all(doubled, 'ctx', split_axis=0, concat_axis=0, tiled=True)]
    ppermute x0 -> x45, waiting for transfers between devices: none -> 155 us  [the longest x12 50.2 us: up(): return lax.ppermute(x, 'ctx', up_perm)]
    another operation x65 -> x0, loops' own time: 82.8 us -> none  [the longest x1 80.8 us: shards(): lax.fori_loop(0, count // half_rows, one_sub, (start_state, start_state))]
    reduce_scatter x1 -> x0, waiting for transfers between devices: 79.8 us -> none  [shards(): lax.psum_scatter(jnp.dot(attended, out_proj, preferred_element_type=jnp.f...]
    ppermute x0 -> x45, starting transfers between devices: none -> 41.5 us  [the longest x12 30.8 us: up(): return lax.ppermute(x, 'ctx', up_perm)]
    dot_general x71 -> x12, matrix products: 80.7 us -> 42 us  [the longest x2 17.1 us: shards(): jnp.dot(hidden, downs[h], preferred_element_type=F32).astype(BF)]
    dynamic_slice x33 -> x1, local copies, waits for them, and re-layouts: 33.6 us -> 0.72 us  [shards(): lax.dynamic_slice_in_dim(out_proj, core * columns, columns, 1)]
    all_to_all x1 -> x3, waiting for transfers between devices: 106 us -> 79.6 us  [the longest x1 39.2 us: shards(): lax.all_to_all(packed, 'ep', split_axis=0, concat_axis=0, tiled=True)]
  transfers between devices with their start and end apart: 4 -> 49, of which waited for: 4 -> 23; matrix products, arithmetic and copies ran while one was open for 0% -> 10% of each run, Pallas kernels for 0% -> 5%
where the time goes in v1:
time: 505 us; the launch traced here: 495 us
  waiting for transfers between devices  293 us (58%)
  starting transfers between devices  60.3 us (12%)
  matrix products  42 us (8%)
  local copies, waits for them, and re-layouts  27 us (5%)
  Pallas kernels  23.8 us (5%)
  blocking collectives  23 us (5%)
  between operations  14.6 us (3%)
  other arithmetic  11.5 us (2%)
    all_gather x1, waiting for transfers between devices, shards(): lax.all_gather(lax.dynamic_slice_in_dim(out_proj, core * columns, columns...  58.8 us
    ppermute x12, waiting for transfers between devices, up(): return lax.ppermute(x, 'ctx', up_perm)  50.2 us
    all_to_all x1, waiting for transfers between devices, shards(): lax.all_to_all(packed, 'ep', split_axis=0, concat_axis=0, tiled=True)  39.2 us
    ppermute x1, waiting for transfers between devices, shards(): downs = (w_down[0], lax.ppermute(w_down[0], 'ep', pair_perm))  32.9 us
    all_to_all x1, waiting for transfers between devices, shards(): lax.all_to_all(expert_out.reshape(n_ep, half * CAP, D), 'ep', split_axis=...  32.3 us
    ppermute x12, starting transfers between devices, up(): return lax.ppermute(x, 'ctx', up_perm)  30.8 us
    pallas_call x5, Pallas kernels, attend(): pl.pallas_call(functools.partial(attention_step, count, first, last), out...  23.8 us
    ppermute x1, waiting for transfers between devices, shards(): gates = (w_gate[0], lax.ppermute(w_gate[0], 'ep', pair_perm))  23.1 us
  transfers between devices with their start and end apart: 49, of which 23 were waited for; matrix products, arithmetic and copies ran while one was open for 10% of the time, Pallas kernels for 5%

profile of v1, /device:TPU:96, one launch (start us, length us, event | category | flops | bytes accessed | tf_op | source)
XLA Modules:
  0.0 495.3 jit_solution(11354447687584294543)
XLA Ops:
  9.4 58.8 %all-gather.4.cloned.1.call-done = bf16[2048,1024]{1,0:T(8,128)(2,1)} async-done(((bf16[128,1024]{1,0:T(8,128)(2,1)}), bf16[2048,1024]{1,0:T(8,128)(2,1)}) %all-gather.4.cloned.1.call-update) | async-done | bytes 4194320 | tf_op jit(solution)/shard_map/all_gather | solution.py:196
  71.5 11.5 %collective-permute-done.refs_2_ = bf16[2048,128]{1,0:T(8,128)(2,1)S(1)} collective-permute-done((bf16[2048,128]{1,0:T(8,128)(2,1)S(1)}, bf16[2048,128]{1,0:T(8,128)(2,1)S(1)}, u32[]{:S(2)}, u32[]{:S(2)}) %collective-permute-start) | collective-permute-done | bytes 524320 | tf_op jit(solution)/shard_map/ppermute | solution.py:162
  86.8 23.0 %all-gather.1 = f32[16,64,16]{1,2,0:T(8,128)S(1)} all-gather(f32[1,64,16]{1,2,0:T(8,128)S(1)} %maximum_bitcast_fusion), channel_id=2, replica_groups=mesh['ctx'=16,'ep'=16] {'ctx'}, dimensions={0}, use_global_device_ids=true | all-gather | bytes 69632 | tf_op jit(solution)/shard_map/all_gather | solution.py:200
  116.3 10.2 %collective-permute-done.2.refs_2_ = bf16[2048,128]{1,0:T(8,128)(2,1)S(1)} collective-permute-done((bf16[2048,128]{1,0:T(8,128)(2,1)}, bf16[2048,128]{1,0:T(8,128)(2,1)S(1)}, u32[]{:S(2)}, u32[]{:S(2)}) %collective-permute-start.2) | collective-permute-done | bytes 524320 | tf_op jit(solution)/shard_map/ppermute | solution.py:162
  134.5 5.5 %collective-permute-done.3 = bf16[1024,128]{1,0:T(8,128)(2,1)S(1)} collective-permute-done((bf16[1024,128]{1,0:T(8,128)(2,1)S(1)}, bf16[1024,128]{1,0:T(8,128)(2,1)S(1)}, u32[]{:S(2)}, u32[]{:S(2)}) %collective-permute-start.3) | collective-permute-done | bytes 262176 | tf_op jit(solution)/shard_map/ppermute | solution.py:162
  148.8 5.6 %shard_map.110 = (f32[3,1,512]{2,1,0:T(1,128)S(1)}, f32[3,1,512]{2,1,0:T(1,128)S(1)}, f32[3,128,512]{2,1,0:T(8,128)S(1)}) custom-call(s32[5]{0:T(128)S(1)} %stack.144.refs_0_, bf16[1024,128]{1,0:T(8,128)(2,1)S(1)} %copy-done.2, bf16[2048,128]{1,0:T(8,128)(2,1)S(1)} %collective-permute-done.refs_2_, bf16[2048,128]{1,0:T(8,128)(2,1)} %collective-permute-done.13.refs_3_, ...), custom_call_target="tpu_custom_call" | custom-call | flops 1073741824 | bytes 2359296 | tf_op jit(solution)/shard_map/pallas_call | solution.py:111
  154.4 5.7 %shard_map.111 = (f32[3,1,512]{2,1,0:T(1,128)S(1)}, f32[3,1,512]{2,1,0:T(1,128)S(1)}, f32[3,128,512]{2,1,0:T(8,128)S(1)}) custom-call(s32[5]{0:T(128)S(1)} %stack.139.refs_0_, bf16[1024,128]{1,0:T(8,128)(2,1)S(1)} %copy-done.2, bf16[2048,128]{1,0:T(8,128)(2,1)} %collective-permute-done.1.refs_2_, bf16[2048,128]{1,0:T(8,128)(2,1)S(1)} %copy-done.8, ...), custom_call_target="tpu_custom_call" | custom-call | flops 1073741824 | bytes 2359296 | tf_op jit(solution)/shard_map/pallas_call | solution.py:111
  160.2 5.8 %shard_map.112 = (f32[3,1,512]{2,1,0:T(1,128)S(1)}, f32[3,1,512]{2,1,0:T(1,128)S(1)}, f32[3,128,512]{2,1,0:T(8,128)S(1)}) custom-call(s32[5]{0:T(128)S(1)} %stack.134.refs_0_, bf16[1024,128]{1,0:T(8,128)(2,1)S(1)} %copy-done.2, bf16[2048,128]{1,0:T(8,128)(2,1)S(1)} %collective-permute-done.2.refs_2_, bf16[2048,128]{1,0:T(8,128)(2,1)} %collective-permute-done.9.refs_3_, ...), custom_call_target="tpu_custom_call" | custom-call | flops 1073741824 | bytes 2359296 | tf_op jit(solution)/shard_map/pallas_call | solution.py:111
  169.7 5.3 %all-to-all-start = ((bf16[16,64,128]{2,1,0:T(8,128)(2,1)}), bf16[16,64,128]{2,1,0:T(8,128)(2,1)S(1)}, u32[]{:S(2)}, u32[]{:S(2)}) async-start(bf16[16,64,128]{2,1,0:T(8,128)(2,1)} %bitcast.17), calls=%async_computation | async-start | bytes 524288 | tf_op jit(solution)/shard_map/all_to_all | solution.py:216
  175.5 8.1 %all-to-all-done = bf16[16,64,128]{2,1,0:T(8,128)(2,1)S(1)} async-done(((bf16[16,64,128]{2,1,0:T(8,128)(2,1)}), bf16[16,64,128]{2,1,0:T(8,128)(2,1)S(1)}, u32[]{:S(2)}, u32[]{:S(2)}) %all-to-all-start) | async-done | bytes 262176 | tf_op jit(solution)/shard_map/all_to_all | solution.py:216
  203.8 4.8 collective-permute-done.22
  242.1 39.2 %all-to-all-done.1 = bf16[16,48,2048]{2,1,0:T(8,128)(2,1)} async-done(((bf16[16,48,2048]{2,1,0:T(8,128)(2,1)}), bf16[16,48,2048]{2,1,0:T(8,128)(2,1)}, u32[]{:S(2)}, u32[]{:S(2)}) %all-to-all-start.1) | async-done | bytes 3145760 | tf_op jit(solution)/shard_map/all_to_all | solution.py:270
  286.0 23.1 %collective-permute-done.33 = bf16[2048,384]{1,0:T(8,128)(2,1)} collective-permute-done((bf16[2048,384]{1,0:T(8,128)(2,1)S(1)}, bf16[2048,384]{1,0:T(8,128)(2,1)}, u32[]{:S(2)}, u32[]{:S(2)}) %collective-permute-start.33) | collective-permute-done | bytes 1572896 | tf_op jit(solution)/shard_map/ppermute | solution.py:192
  309.1 5.3 %fusion.50 = f32[768,384]{1,0:T(8,128)} fusion(bf16[768,2048]{1,0:T(8,128)(2,1)} %bitcast.48, bf16[2048,384]{1,0:T(8,128)(2,1)} %collective-permute-done.33), kind=kOutput, calls=%fused_computation.126 | convolution fusion | flops 1207959552 | bytes 5898240 | tf_op jit(solution)/shard_map/dot_general | solution.py:274
  314.4 7.8 %convolution_convert_fusion.1 = bf16[768,2048]{1,0:T(8,128)(2,1)} fusion(bf16[768,2048]{1,0:T(8,128)(2,1)} %bitcast.48, f32[768,384]{1,0:T(8,128)} %fusion.40, bf16[1,384,2048]{2,1,0:T(8,128)(2,1)} %param.19, bf16[1,2048,384]{2,1,0:T(8,128)(2,1)S(1)} %copy-done.25), kind=kOutput, calls=%fused_computation.8 | convolution fusion | flops 2419261440 | bytes 10616832 | tf_op jit(solution)/shard_map/dot_general | solution.py:277
  322.3 20.5 %collective-permute-done.34 = bf16[2048,384]{1,0:T(8,128)(2,1)} collective-permute-done((bf16[2048,384]{1,0:T(8,128)(2,1)}, bf16[2048,384]{1,0:T(8,128)(2,1)}, u32[]{:S(2)}, u32[]{:S(2)}) %collective-permute-start.34) | collective-permute-done | bytes 1572896 | tf_op jit(solution)/shard_map/ppermute | solution.py:193
  342.8 32.9 %collective-permute-done.35 = bf16[384,2048]{1,0:T(8,128)(2,1)} collective-permute-done((bf16[384,2048]{1,0:T(8,128)(2,1)}, bf16[384,2048]{1,0:T(8,128)(2,1)}, u32[]{:S(2)}, u32[]{:S(2)}) %collective-permute-start.35) | collective-permute-done | bytes 1572896 | tf_op jit(solution)/shard_map/ppermute | solution.py:194
  375.7 9.2 %add_convert_fusion = bf16[768,2048]{1,0:T(8,128)(2,1)} fusion(bf16[768,2048]{1,0:T(8,128)(2,1)} %convolution_convert_fusion.1, bf16[384,2048]{1,0:T(8,128)(2,1)} %collective-permute-done.35, f32[768,384]{1,0:T(8,128)} %fusion.50, bf16[768,2048]{1,0:T(8,128)(2,1)} %bitcast.48, bf16[2048,384]{1,0:T(8,128)(2,1)} %collective-permute-done.34), kind=kOutput, calls=%fused_computation.1 | convolution fusion | flops 2425552896 | bytes 13762560 | tf_op jit(solution)/shard_map/dot_general | solution.py:277
  384.9 8.9 %all-to-all-start.2 = ((bf16[16,48,2048]{2,1,0:T(8,128)(2,1)}), bf16[16,48,2048]{2,1,0:T(8,128)(2,1)}, u32[]{:S(2)}, u32[]{:S(2)}) async-start(bf16[16,48,2048]{2,1,0:T(8,128)(2,1)} %bitcast.183), calls=%async_computation.2 | async-start | bytes 6291456 | tf_op jit(solution)/shard_map/all_to_all | solution.py:279
  404.2 32.3 %all-to-all-done.2 = bf16[16,48,2048]{2,1,0:T(8,128)(2,1)} async-done(((bf16[16,48,2048]{2,1,0:T(8,128)(2,1)}), bf16[16,48,2048]{2,1,0:T(8,128)(2,1)}, u32[]{:S(2)}, u32[]{:S(2)}) %all-to-all-start.2) | async-done | bytes 3145760 | tf_op jit(solution)/shard_map/all_to_all | solution.py:279
  460.3 5.1 %collective-permute-done.38 = bf16[64,2048]{1,0:T(8,128)(2,1)S(1)} collective-permute-done((bf16[64,2048]{1,0:T(8,128)(2,1)S(1)}, bf16[64,2048]{1,0:T(8,128)(2,1)S(1)}, u32[]{:S(2)}, u32[]{:S(2)}) %collective-permute-start.38) | collective-permute-done | bytes 262176 | tf_op jit(solution)/shard_map/ppermute | solution.py:165
  465.5 7.8 %collective-permute-done.39 = bf16[64,2048]{1,0:T(8,128)(2,1)S(1)} collective-permute-done((bf16[64,2048]{1,0:T(8,128)(2,1)S(1)}, bf16[64,2048]{1,0:T(8,128)(2,1)S(1)}, u32[]{:S(2)}, u32[]{:S(2)}) %collective-permute-start.39) | collective-permute-done | bytes 262176 | tf_op jit(solution)/shard_map/ppermute | solution.py:165
  475.6 5.2 %collective-permute-done.43 = bf16[64,2048]{1,0:T(8,128)(2,1)S(1)} collective-permute-done((bf16[64,2048]{1,0:T(8,128)(2,1)S(1)}, bf16[64,2048]{1,0:T(8,128)(2,1)S(1)}, u32[]{:S(2)}, u32[]{:S(2)}) %collective-permute-start.43) | collective-permute-done | bytes 262176 | tf_op jit(solution)/shard_map/ppermute | solution.py:162
  481.3 6.0 %collective-permute-done.44 = bf16[64,2048]{1,0:T(8,128)(2,1)S(1)} collective-permute-done((bf16[64,2048]{1,0:T(8,128)(2,1)S(1)}, bf16[64,2048]{1,0:T(8,128)(2,1)S(1)}, u32[]{:S(2)}, u32[]{:S(2)}) %collective-permute-start.44) | collective-permute-done | bytes 262176 | tf_op jit(solution)/shard_map/ppermute | solution.py:162
  (227 shorter events, 133.0 us)
Async XLA Ops:
  6.5 61.7 %all-gather.4.cloned.1.call-start = ((), (), s32[]{:S(2)}) async-start(), calls=%async_computation.3 | async-start | bytes 4456448 | tf_op jit(solution)/shard_map/all_gather | solution.py:196
  68.3 118.4 %collective-permute-start.16 = (bf16[2048,1024]{1,0:T(8,128)(2,1)}, bf16[2048,1024]{1,0:T(8,128)(2,1)}, u32[]{:S(2)}, u32[]{:S(2)}) collective-permute-start(bf16[2048,1024]{1,0:T(8,128)(2,1)} %all-gather.4.cloned.1.call-done), channel_id=1, source_target_pairs={{0,16},{16,0},{32,48},{48,32},{64,80},{80,64},{96,112},{112,96},{1... | collective-permute-start | bytes 12582920 | tf_op jit(solution)/shard_map/ppermute | solution.py:168
  68.3 14.7 %collective-permute-start = (bf16[2048,128]{1,0:T(8,128)(2,1)S(1)}, bf16[2048,128]{1,0:T(8,128)(2,1)S(1)}, u32[]{:S(2)}, u32[]{:S(2)}) collective-permute-start(bf16[2048,128]{1,0:T(8,128)(2,1)S(1)} %pad_maximum_fusion.2.refs_2_), channel_id=1, source_target_pairs={{0,32},{16,48},{32,64},{48,80},{64,96},{80,112},{96,128},{112,144}... | collective-permute-start | bytes 1572872 | tf_op jit(solution)/shard_map/ppermute | solution.py:162
  71.1 15.6 %collective-permute-start.4 = (bf16[2048,128]{1,0:T(8,128)(2,1)S(1)}, bf16[2048,128]{1,0:T(8,128)(2,1)S(1)}, u32[]{:S(2)}, u32[]{:S(2)}) collective-permute-start(bf16[2048,128]{1,0:T(8,128)(2,1)S(1)} %pad_maximum_fusion.2.refs_2_), channel_id=1, source_target_pairs={{0,224},{16,240},{32,0},{48,16},{64,32},{80,48},{96,64},{112,80},{... | collective-permute-start | bytes 1572872 | tf_op jit(solution)/shard_map/ppermute | solution.py:165
  71.1 59.3 %collective-permute-start.15 = (bf16[2048,128]{1,0:T(8,128)(2,1)S(1)}, bf16[2048,128]{1,0:T(8,128)(2,1)S(1)}, u32[]{:S(2)}, u32[]{:S(2)}) collective-permute-start(bf16[2048,128]{1,0:T(8,128)(2,1)S(1)} %pad_maximum_fusion.2.refs_2_), channel_id=1, source_target_pairs={{0,16},{16,0},{32,48},{48,32},{64,80},{80,64},{96,112},{112,96},{1... | collective-permute-start | bytes 1572872 | tf_op jit(solution)/shard_map/ppermute | solution.py:168
  83.0 27.5 %collective-permute-start.1 = (bf16[2048,128]{1,0:T(8,128)(2,1)S(1)}, bf16[2048,128]{1,0:T(8,128)(2,1)}, u32[]{:S(2)}, u32[]{:S(2)}) collective-permute-start(bf16[2048,128]{1,0:T(8,128)(2,1)S(1)} %collective-permute-done.refs_2_), channel_id=1, source_target_pairs={{0,32},{16,48},{32,64},{48,80},{64,96},{80,112},{96,128},{112,144}... | collective-permute-start | bytes 1572872 | tf_op jit(solution)/shard_map/ppermute | solution.py:162
  86.7 28.0 %collective-permute-start.5 = (bf16[2048,128]{1,0:T(8,128)(2,1)S(1)}, bf16[2048,128]{1,0:T(8,128)(2,1)}, u32[]{:S(2)}, u32[]{:S(2)}) collective-permute-start(bf16[2048,128]{1,0:T(8,128)(2,1)S(1)} %collective-permute-done.4.refs_4_), channel_id=1, source_target_pairs={{0,224},{16,240},{32,0},{48,16},{64,32},{80,48},{96,64},{112,80},{... | collective-permute-start | bytes 1572872 | tf_op jit(solution)/shard_map/ppermute | solution.py:165
  110.5 15.9 %collective-permute-start.2 = (bf16[2048,128]{1,0:T(8,128)(2,1)}, bf16[2048,128]{1,0:T(8,128)(2,1)S(1)}, u32[]{:S(2)}, u32[]{:S(2)}) collective-permute-start(bf16[2048,128]{1,0:T(8,128)(2,1)} %collective-permute-done.1.refs_2_), channel_id=1, source_target_pairs={{0,32},{16,48},{32,64},{48,80},{64,96},{80,112},{96,128},{112,144}... | collective-permute-start | bytes 1572872 | tf_op jit(solution)/shard_map/ppermute | solution.py:162
  114.6 19.1 %collective-permute-start.13 = (bf16[2048,128]{1,0:T(8,128)(2,1)S(1)}, bf16[2048,128]{1,0:T(8,128)(2,1)}, u32[]{:S(2)}, u32[]{:S(2)}) collective-permute-start(bf16[2048,128]{1,0:T(8,128)(2,1)S(1)} %collective-permute-done.refs_2_), channel_id=1, source_target_pairs={{0,16},{16,0},{32,48},{48,32},{64,80},{80,64},{96,112},{112,96},{1... | collective-permute-start | bytes 1572872 | tf_op jit(solution)/shard_map/ppermute | solution.py:168
  114.7 15.7 %collective-permute-start.6 = (bf16[2048,128]{1,0:T(8,128)(2,1)}, bf16[2048,128]{1,0:T(8,128)(2,1)S(1)}, u32[]{:S(2)}, u32[]{:S(2)}) collective-permute-start(bf16[2048,128]{1,0:T(8,128)(2,1)} %collective-permute-done.5.refs_4_), channel_id=1, source_target_pairs={{0,224},{16,240},{32,0},{48,16},{64,32},{80,48},{96,64},{112,80},{... | collective-permute-start | bytes 1572872 | tf_op jit(solution)/shard_map/ppermute | solution.py:165
  126.5 13.6 %collective-permute-start.14 = (bf16[2048,128]{1,0:T(8,128)(2,1)S(1)}, bf16[2048,128]{1,0:T(8,128)(2,1)}, u32[]{:S(2)}, u32[]{:S(2)}) collective-permute-start(bf16[2048,128]{1,0:T(8,128)(2,1)S(1)} %collective-permute-done.4.refs_4_), channel_id=1, source_target_pairs={{0,16},{16,0},{32,48},{48,32},{64,80},{80,64},{96,112},{112,96},{1... | collective-permute-start | bytes 1572872 | tf_op jit(solution)/shard_map/ppermute | solution.py:168
  140.0 14.4 %collective-permute-start.12 = (bf16[2048,128]{1,0:T(8,128)(2,1)}, bf16[2048,128]{1,0:T(8,128)(2,1)}, u32[]{:S(2)}, u32[]{:S(2)}) collective-permute-start(bf16[2048,128]{1,0:T(8,128)(2,1)} %collective-permute-done.5.refs_4_), channel_id=1, source_target_pairs={{0,16},{16,0},{32,48},{48,32},{64,80},{80,64},{96,112},{112,96},{1... | collective-permute-start | bytes 1572872 | tf_op jit(solution)/shard_map/ppermute | solution.py:168
  140.0 20.1 %collective-permute-start.10 = (bf16[2048,128]{1,0:T(8,128)(2,1)S(1)}, bf16[2048,128]{1,0:T(8,128)(2,1)}, u32[]{:S(2)}, u32[]{:S(2)}) collective-permute-start(bf16[2048,128]{1,0:T(8,128)(2,1)S(1)} %collective-permute-done.6.refs_4_), channel_id=1, source_target_pairs={{0,16},{16,0},{32,48},{48,32},{64,80},{80,64},{96,112},{112,96},{1... | collective-permute-start | bytes 1572872 | tf_op jit(solution)/shard_map/ppermute | solution.py:168
  142.8 17.3 %collective-permute-start.9 = (bf16[2048,128]{1,0:T(8,128)(2,1)S(1)}, bf16[2048,128]{1,0:T(8,128)(2,1)}, u32[]{:S(2)}, u32[]{:S(2)}) collective-permute-start(bf16[2048,128]{1,0:T(8,128)(2,1)S(1)} %collective-permute-done.2.refs_2_), channel_id=1, source_target_pairs={{0,16},{16,0},{32,48},{48,32},{64,80},{80,64},{96,112},{112,96},{1... | collective-permute-start | bytes 1572872 | tf_op jit(solution)/shard_map/ppermute | solution.py:168
  143.7 22.3 %collective-permute-start.8 = (bf16[2048,128]{1,0:T(8,128)(2,1)S(1)}, bf16[2048,128]{1,0:T(8,128)(2,1)S(1)}, u32[]{:S(2)}, u32[]{:S(2)}) collective-permute-start(bf16[2048,128]{1,0:T(8,128)(2,1)S(1)} %constant_dynamic-update-slice_fusion.refs_2_), channel_id=1, source_target_pairs={{0,16},{16,0},{32,48},{48,32},{64,80},{80,64},{96,112},{112,96},{1... | collective-permute-start | bytes 1572872 | tf_op jit(solution)/shard_map/ppermute | solution.py:168
  169.7 13.9 %all-to-all-start = ((bf16[16,64,128]{2,1,0:T(8,128)(2,1)}), bf16[16,64,128]{2,1,0:T(8,128)(2,1)S(1)}, u32[]{:S(2)}, u32[]{:S(2)}) async-start(bf16[16,64,128]{2,1,0:T(8,128)(2,1)} %bitcast.17), calls=%async_computation | async-start | bytes 524288 | tf_op jit(solution)/shard_map/all_to_all | solution.py:216
  199.8 12.7 %collective-permute-start.19 = (bf16[64,2048]{1,0:T(8,128)(2,1)S(1)}, bf16[64,2048]{1,0:T(8,128)(2,1)S(1)}, u32[]{:S(2)}, u32[]{:S(2)}) collective-permute-start(bf16[64,2048]{1,0:T(8,128)(2,1)S(1)} %collective-permute-done.18), channel_id=1, source_target_pairs={{0,16},{16,0},{32,48},{48,32},{64,80},{80,64},{96,112},{112,96},{1... | collective-permute-start | bytes 786440 | tf_op jit(solution)/shard_map/ppermute | solution.py:168
  208.6 14.1 %collective-permute-start.23 = (bf16[64,2048]{1,0:T(8,128)(2,1)S(1)}, bf16[64,2048]{1,0:T(8,128)(2,1)S(1)}, u32[]{:S(2)}, u32[]{:S(2)}) collective-permute-start(bf16[64,2048]{1,0:T(8,128)(2,1)S(1)} %collective-permute-done.22), channel_id=1, source_target_pairs={{0,16},{16,0},{32,48},{48,32},{64,80},{80,64},{96,112},{112,96},{1... | collective-permute-start | bytes 786440 | tf_op jit(solution)/shard_map/ppermute | solution.py:168
  212.6 13.9 %collective-permute-start.25 = (bf16[64,2048]{1,0:T(8,128)(2,1)S(1)}, bf16[64,2048]{1,0:T(8,128)(2,1)S(1)}, u32[]{:S(2)}, u32[]{:S(2)}) collective-permute-start(bf16[64,2048]{1,0:T(8,128)(2,1)S(1)} %collective-permute-done.24), channel_id=1, source_target_pairs={{0,16},{16,0},{32,48},{48,32},{64,80},{80,64},{96,112},{112,96},{1... | collective-permute-start | bytes 786440 | tf_op jit(solution)/shard_map/ppermute | solution.py:168
  233.5 47.8 %all-to-all-start.1 = ((bf16[16,48,2048]{2,1,0:T(8,128)(2,1)}), bf16[16,48,2048]{2,1,0:T(8,128)(2,1)}, u32[]{:S(2)}, u32[]{:S(2)}) async-start(bf16[16,48,2048]{2,1,0:T(8,128)(2,1)} %bitcast.47), calls=%async_computation.1 | async-start | bytes 6291456 | tf_op jit(solution)/shard_map/all_to_all | solution.py:270
  238.1 71.0 %collective-permute-start.33 = (bf16[2048,384]{1,0:T(8,128)(2,1)S(1)}, bf16[2048,384]{1,0:T(8,128)(2,1)}, u32[]{:S(2)}, u32[]{:S(2)}) collective-permute-start(bf16[2048,384]{1,0:T(8,128)(2,1)S(1)} %bitcast.190), channel_id=1, source_target_pairs={{0,1},{1,0},{2,3},{3,2},{4,5},{5,4},{6,7},{7,6},{8,9},{9,8},{10,11... | collective-permute-start | bytes 4718600 | tf_op jit(solution)/shard_map/ppermute | solution.py:192
  239.9 102.8 %collective-permute-start.34 = (bf16[2048,384]{1,0:T(8,128)(2,1)}, bf16[2048,384]{1,0:T(8,128)(2,1)}, u32[]{:S(2)}, u32[]{:S(2)}) collective-permute-start(bf16[2048,384]{1,0:T(8,128)(2,1)} %bitcast.191), channel_id=1, source_target_pairs={{0,1},{1,0},{2,3},{3,2},{4,5},{5,4},{6,7},{7,6},{8,9},{9,8},{10,11... | collective-permute-start | bytes 4718600 | tf_op jit(solution)/shard_map/ppermute | solution.py:193
  240.2 135.5 %collective-permute-start.35 = (bf16[384,2048]{1,0:T(8,128)(2,1)}, bf16[384,2048]{1,0:T(8,128)(2,1)}, u32[]{:S(2)}, u32[]{:S(2)}) collective-permute-start(bf16[384,2048]{1,0:T(8,128)(2,1)} %bitcast.192), channel_id=1, source_target_pairs={{0,1},{1,0},{2,3},{3,2},{4,5},{5,4},{6,7},{7,6},{8,9},{9,8},{10,11... | collective-permute-start | bytes 4718600 | tf_op jit(solution)/shard_map/ppermute | solution.py:194
  384.9 51.6 %all-to-all-start.2 = ((bf16[16,48,2048]{2,1,0:T(8,128)(2,1)}), bf16[16,48,2048]{2,1,0:T(8,128)(2,1)}, u32[]{:S(2)}, u32[]{:S(2)}) async-start(bf16[16,48,2048]{2,1,0:T(8,128)(2,1)} %bitcast.183), calls=%async_computation.2 | async-start | bytes 6291456 | tf_op jit(solution)/shard_map/all_to_all | solution.py:279
  (51 other events, 579.3 us)
Sparse Core Ops, SparseCore 0:
  9.8 58.4 all-gather.3
